TPU v7x, 32 devices: a whole 2x2x4 slice. The times are simulated.
32 devices in a mesh: section: 8 (over y, x, core), rep: 4 (over z).
Axes of the slice: x: 2, y: 2, z: 4, core: 2. Of those that a mesh axis runs over, the one named last changes fastest.
Arguments:
- tokens: bfloat16 [8, 4, 256, 1024], P('section', 'rep'), may hold values from -6 to 6
- assign: int32 [8, 4, 256, 1], P('section', 'rep'), may hold values from 0 to 7; in each aligned block of 256 rows (0 to 255, 256 to 511, ..., all dimensions but the last counted through in order) at most 48 rows name the same one
- route_mask: int32 [8], replicated, may hold values from 1 to 3
- match_mask: int32 [8], replicated, may hold values from 1 to 3
- gate_weight: bfloat16 [8, 4, 1024, 256], P('section', 'rep'), may hold values from -0.1875 to 0.1875
- up_weight: bfloat16 [8, 4, 1024, 256], P('section', 'rep'), may hold values from -0.1875 to 0.1875
- down_weight: bfloat16 [8, 4, 256, 1024], P('section', 'rep'), may hold values from -0.375 to 0.375
- slow_down: bfloat16 [8, 4, 256, 1024], P('section', 'rep'), may hold values from -4 to 4
- momentum: bfloat16 [8, 4, 256, 1024], P('section', 'rep'), may hold values from -4 to 4
- slot_cot: bfloat16 [8, 4, 8, 48, 1024], P('section', 'rep'), may hold values from -6 to 6
Outputs:
- input_grad: bfloat16 [8, 4, 256, 1024], P('section', 'rep')
- new_slow: bfloat16 [8, 4, 256, 1024], P('section', 'rep')
Inputs may be any that keep to these rules, and one draw needn't show every extreme that they name: `assign`: no expert is named by more than 48 rows of one device, and in every draw some device has 48 rows for one expert. Rows that replica r of any section sends to expert e are processed by replica r XOR route_mask[e] of that expert. Replica r of section s is matched with replica r XOR match_mask[s].
All inputs are finite; a program needn't handle non-finite values.
Results may differ from a plain program's by a relative error of at most 0.012.
Values may be sent and summed in bfloat16 or wider, within the bound.
No kernel may reach another device: no remote copies, remote signals or barrier semaphores. Data moves between devices by JAX's collectives and lax.ppermute only.
A program may use at most 64 MiB of HBM per device.

v0:
```python
import jax
import jax.numpy as jnp
from jax import lax
from jax.sharding import PartitionSpec as P

inner_rate = 0.05
pull_rate = 0.25
moment_rate = 0.9
outer_rate = 0.7

OUTWARD = [(1, 0), (2, 3)]
INWARD = [(0, 1), (3, 2)]
ACROSS = [(1, 2), (2, 1)]


def from_partner(value, distance):
    pairs = [(source, source ^ 2**distance) for source in range(lax.axis_size("rep"))]
    return lax.ppermute(value, "rep", pairs)


def bit_of(mask, index):
    return jnp.bitwise_and(jnp.right_shift(mask, index), 1) == 1


def route(value, mask, bits):
    for index in bits:
        value = jnp.where(bit_of(mask, index), from_partner(value, index), value)
    return value


def after(value, *earlier):
    return lax.optimization_barrier((value, *earlier))[0]


def slot_table(expert_ids, sections, capacity):
    expert_hot = (expert_ids[:, None] == jnp.arange(sections, dtype=jnp.int32)[None, :]).astype(
        jnp.int32
    )
    position = jnp.sum((jnp.cumsum(expert_hot, axis=0) - 1) * expert_hot, axis=1)
    slot_index = expert_ids * capacity + position
    return (
        slot_index[:, None] == jnp.arange(sections * capacity, dtype=jnp.int32)[None, :]
    ).astype(jnp.bfloat16)


def stacked(wide, width):
    return jnp.concatenate(jnp.split(wide, wide.shape[1] // width, axis=1), axis=0)


def side_by_side(tall):
    return jnp.concatenate(jnp.split(tall, tall.shape[0] // tall.shape[1], axis=0), axis=1)


class FourInLine:
    def __init__(self, gate, up, down, static_part, mask):
        replica = lax.axis_index("rep")
        self.inner = (replica == 1) | (replica == 2)
        self.near, self.far = mask == 1, mask == 3
        self.gate, self.up, self.down = gate, up, down
        self.static_part = static_part

    def forward(self, bits):
        self.up_side = lax.ppermute(self.up, "rep", INWARD)
        self.gate_hub = lax.ppermute(self.gate, "rep", ACROSS)
        inner, self.near, self.far, *bits = lax.optimization_barrier(
            (self.inner, self.near, self.far, *bits)
        )
        send = lax.optimization_barrier(jnp.where(inner, self.static_part, self.gate))
        self.one = from_partner(send, 0)
        side, self.gate_hub, self.near, self.far = lax.optimization_barrier(
            (self.up_side, self.gate_hub, self.near, self.far)
        )
        first = jnp.where(self.far, side, self.up)
        second = jnp.where(self.far, self.up, side)
        first_in = lax.ppermute(first, "rep", ACROSS)
        self.quiet, self.first_in = first, first_in
        self.gate_edge = lax.ppermute(self.one, "rep", ACROSS)
        self.second = second
        return bits

    def handed_up(self, earlier):
        first_in = after(self.first_in, *earlier)
        send = jnp.where(self.inner, jnp.where(self.near, self.up, first_in), self.down)
        self.two = from_partner(send, 0)
        self.up_hub = lax.ppermute(after(self.second, send), "rep", ACROSS)
        self.later = send

    def handed_gate(self, earlier):
        gate_edge = after(self.gate_edge, self.later, *earlier)
        gate_out = jnp.where(
            self.near, self.gate, jnp.where(self.far, gate_edge, self.gate_hub)
        )
        send = jnp.where(self.inner, gate_out, self.static_part)
        self.three = from_partner(send, 0)
        two = after(self.two, send)
        first = jnp.where(self.far, two, self.down)
        second = jnp.where(self.far, self.down, two)
        self.down_first = lax.ppermute(first, "rep", ACROSS)
        gate_in = jnp.where(
            self.near, self.one, jnp.where(self.far, self.gate_hub, self.gate_edge)
        )
        two, up_hub = lax.optimization_barrier((two, self.up_hub, first))[:2]
        self.second_down = second
        up_in = jnp.where(self.near, self.up_side, up_hub)
        self.gate_in = gate_in
        return jnp.where(self.inner, up_in, two)

    def gate_here(self, earlier):
        three = after(self.three, *earlier)
        static_in = jnp.where(self.inner, three, self.one)
        return lax.optimization_barrier(jnp.where(self.inner, self.gate_in, three)), static_in

    def swap_down(self, earlier):
        second = after(self.second_down, *earlier)
        self.down_hub = lax.ppermute(second, "rep", ACROSS)

    def handed_down(self, earlier):
        send = jnp.where(self.near, self.down, after(self.down_first, *earlier))
        self.four = lax.ppermute(send, "rep", OUTWARD)
        return send

    def down_here(self, earlier):
        down_hub = after(self.down_hub, *earlier)
        down_in = jnp.where(self.near, self.two, down_hub)
        return jnp.where(self.inner, down_in, self.four)


def on_device(
    tokens,
    assign,
    route_mask,
    match_mask,
    gate_weight,
    up_weight,
    down_weight,
    slow_down,
    momentum,
    slot_cot,
):
    sections = lax.axis_size("section")
    levels = lax.axis_size("rep").bit_length() - 1
    section_here = lax.axis_index("section")
    token_rows = tokens[0, 0]
    expert_ids = assign[0, 0, :, 0]
    capacity = slot_cot.shape[3]
    model_width = token_rows.shape[1]
    masks_here = lax.dynamic_index_in_dim(
        jnp.stack([route_mask, match_mask]), section_here, axis=1, keepdims=False
    )
    own_mask, match = masks_here[0], masks_here[1]
    match_mine = jnp.bitwise_xor(own_mask, match)
    upward = list(range(levels))
    bits = [bit_of(mask, index) for mask in (own_mask, match_mine, match) for index in upward]
    contract = (((1,), (1,)), ((), ()))
    hidden_width = gate_weight.shape[3]

    gate_raw, up_raw, down_raw = gate_weight[0, 0], up_weight[0, 0], down_weight[0, 0]
    slow_float = slow_down[0, 0].astype(jnp.float32)
    down_float = down_raw.astype(jnp.float32)
    static_part = ((0.5 - pull_rate) * slow_float - 0.5 * down_float).astype(jnp.bfloat16)

    selector = slot_table(expert_ids, sections, capacity)
    placed = lax.dot_general(
        selector, token_rows, (((0,), (0,)), ((), ())), preferred_element_type=jnp.float32
    )
    dispatched = placed.astype(jnp.bfloat16).reshape(sections, capacity, model_width)

    line = None
    if levels == 2:
        line = FourInLine(
            gate_raw,
            up_raw,
            stacked(down_raw, hidden_width),
            stacked(lax.optimization_barrier(static_part), hidden_width),
            own_mask,
        )
        bits = line.forward(bits)
        dispatched = after(dispatched, line.quiet)
        line.handed_up((dispatched,))
    arrived = lax.all_to_all(dispatched, "section", split_axis=0, concat_axis=0, tiled=True)
    rows = arrived.reshape(-1, model_width)
    cotangent = slot_cot[0, 0].reshape(-1, model_width)
    if line is not None:
        up_mat = line.handed_gate((rows,))
    else:
        gate_mat, up_mat, down_mat = [
            route(weight, own_mask, upward) for weight in (gate_raw, up_raw, down_raw)
        ]
        static_in = from_partner(static_part, 0)

    up_act = jnp.dot(rows, up_mat, preferred_element_type=jnp.float32)
    if line is not None:
        gate_mat, static_in = line.gate_here((up_act,))
        static_in = side_by_side(static_in)
    gate_act = jnp.dot(rows, gate_mat, preferred_element_type=jnp.float32)
    sigmoid_gate = jax.nn.sigmoid(gate_act)
    hidden = (gate_act * sigmoid_gate * up_act).astype(jnp.bfloat16)
    down_grad = lax.dot_general(
        hidden, cotangent, (((0,), (0,)), ((), ())), preferred_element_type=jnp.float32
    ).astype(jnp.bfloat16)

    if line is not None:
        line.swap_down((down_grad,))

    own_bits, mine_bits, match_bits = [
        bits[number * levels : (number + 1) * levels] for number in range(3)
    ]
    lower, top = upward[:-1], levels - 1
    down_grad_in = from_partner(down_grad, 0)
    if line is not None:
        sent = line.handed_down((down_grad,))
        static_in = after(static_in, sent)
        down_grad_in = after(down_grad_in, static_in, line.down_hub)
    own_routed, match_routed, static_routed = down_grad, down_grad, static_part
    for index in lower:
        if index == 0:
            own_in, match_in, static_here = down_grad_in, down_grad_in, static_in
        else:
            own_in = from_partner(own_routed, index)
            match_in = from_partner(match_routed, index)
            static_here = from_partner(static_routed, index)
        own_routed = jnp.where(own_bits[index], own_in, own_routed)
        match_routed = jnp.where(mine_bits[index], match_in, match_routed)
        static_routed = jnp.where(match_bits[index], static_here, static_routed)

    def combined(side, static_routed, own_routed, match_routed):
        def pick(bit, value):
            return jnp.where(bit == side, value.astype(jnp.float32), 0.0)

        return pick(match_bits[top], static_routed) + 0.5 * inner_rate * (
            pick(own_bits[top], own_routed) + pick(mine_bits[top], match_routed)
        )

    crossing_out = combined(True, static_routed, own_routed, match_routed).astype(jnp.bfloat16)
    crossing = from_partner(crossing_out, top)
    slow_float = after(slow_down[0, 0], crossing_out).astype(jnp.float32)
    staying = combined(False, static_routed, own_routed, match_routed)
    outer_here = (0.5 + pull_rate) * slow_float - 0.5 * down_float + staying
    pull = outer_rate * (1.0 + moment_rate)
    kept = (
        slow_float
        - pull * outer_here
        - (outer_rate * moment_rate * moment_rate) * momentum[0, 0].astype(jnp.float32)
    )
    kept = after(kept, crossing_out)
    new_slow = (kept - pull * crossing.astype(jnp.float32)).astype(jnp.bfloat16)

    if line is not None:
        down_mat = side_by_side(line.down_here((crossing_out,)))
    hidden_grad = lax.dot_general(
        cotangent, down_mat, contract, preferred_element_type=jnp.float32
    )
    gate_grad = (
        hidden_grad * up_act * sigmoid_gate * (1.0 + gate_act * (1.0 - sigmoid_gate))
    ).astype(jnp.bfloat16)
    up_grad = (hidden_grad * gate_act * sigmoid_gate).astype(jnp.bfloat16)
    slot_grad = (
        lax.dot_general(gate_grad, gate_mat, contract, preferred_element_type=jnp.float32)
        + lax.dot_general(up_grad, up_mat, contract, preferred_element_type=jnp.float32)
    ).astype(jnp.bfloat16)
    slot_grad = slot_grad.reshape(sections, capacity, model_width)
    returned = lax.all_to_all(slot_grad, "section", split_axis=0, concat_axis=0, tiled=True)
    input_grad = jnp.dot(
        selector, returned.reshape(-1, model_width), preferred_element_type=jnp.float32
    ).astype(jnp.bfloat16)
    return (input_grad[None, None], new_slow[None, None])


def solution(mesh):
    in_specs = (
        P("section", "rep", None, None),
        P("section", "rep", None, None),
        P(),
        P(),
        P("section", "rep", None, None),
        P("section", "rep", None, None),
        P("section", "rep", None, None),
        P("section", "rep", None, None),
        P("section", "rep", None, None),
        P("section", "rep", None, None, None),
    )
    out_specs = (P("section", "rep", None, None), P("section", "rep", None, None))
    return jax.shard_map(
        on_device, mesh=mesh, in_specs=in_specs, out_specs=out_specs, check_vma=False
    )
```

profile of v0, /device:TPU:0, one launch (start us, length us, event | category | flops | bytes accessed | tf_op | source)
XLA Modules:
  0.0 109.5 jit_solution(7272883554673725024)
XLA Ops:
  0.6 5.1 %collective-permute-start = (bf16[1024,256]{1,0:T(8,128)(2,1)}, bf16[1024,256]{1,0:T(8,128)(2,1)S(1)}, u32[]{:S(2)}, u32[]{:S(2)}) collective-permute-start(bf16[1024,256]{1,0:T(8,128)(2,1)} %bitcast.63), channel_id=1, source_target_pairs={{0,1},{3,2},{4,5},{7,6},{8,9},{11,10},{12,13},{15,14},{16,17},{19,... | collective-permute-start | bytes 1572872 | tf_op jit(solution)/shard_map/ppermute | solution.py:63
  12.9 1.4 %subtract_convert_fusion.1 = bf16[256,1024]{1,0:T(8,128)(2,1)S(1)} fusion(bf16[1,1,256,1024]{3,2,1,0:T(8,128)(2,1)} %param.17, bf16[1,1,256,1024]{3,2,1,0:T(8,128)(2,1)} %param.16), kind=kLoop, calls=%fused_computation.26 | loop fusion | flops 1572864 | bytes 1572864 | tf_op jit(solution)/shard_map/convert_element_type | solution.py:160
  15.4 2.1 %collective-permute-start.4 = (bf16[1024,256]{1,0:T(8,128)(2,1)}, bf16[1024,256]{1,0:T(8,128)(2,1)}, u32[]{:S(2)}, u32[]{:S(2)}) collective-permute-start(bf16[1024,256]{1,0:T(8,128)(2,1)} %broadcast_select_fusion.3), channel_id=1, source_target_pairs={{0,1},{1,0},{2,3},{3,2},{4,5},{5,4},{6,7},{7,6},{8,9},{9,8},{10,11... | collective-permute-start | bytes 1572872 | tf_op jit(solution)/shard_map/ppermute | solution.py:18
  20.5 1.6 %collective-permute-start.2 = (bf16[1024,256]{1,0:T(8,128)(2,1)}, bf16[1024,256]{1,0:T(8,128)(2,1)}, u32[]{:S(2)}, u32[]{:S(2)}) collective-permute-start(bf16[1024,256]{1,0:T(8,128)(2,1)} %get-tuple-element.63), channel_id=1, source_target_pairs={{1,2},{2,1},{5,6},{6,5},{9,10},{10,9},{13,14},{14,13},{17,18},{18,... | collective-permute-start | bytes 1572872 | tf_op jit(solution)/shard_map/ppermute | solution.py:75
  22.1 1.4 %convolution_convert_fusion = bf16[384,1024]{1,0:T(8,128)(2,1)} fusion(bf16[1,1,256,1024]{3,2,1,0:T(8,128)(2,1)S(1)} %copy-done.16, s32[256]{0:T(256)S(1)} %multiply_add_fusion), kind=kOutput, calls=%fused_computation.1 | convolution fusion | flops 201818112 | bytes 1311744 | tf_op jit(solution)/shard_map/dot_general | solution.py:163
  23.4 3.7 %all-to-all-start = ((bf16[8,48,1024]{2,1,0:T(8,128)(2,1)}), bf16[8,48,1024]{2,1,0:T(8,128)(2,1)S(1)}, u32[]{:S(2)}, u32[]{:S(2)}) async-start(bf16[8,48,1024]{2,1,0:T(8,128)(2,1)} %bitcast.17), calls=%async_computation | async-start | bytes 1572864 | tf_op jit(solution)/shard_map/all_to_all | solution.py:180
  27.2 2.4 %collective-permute-done.4 = bf16[1024,256]{1,0:T(8,128)(2,1)} collective-permute-done((bf16[1024,256]{1,0:T(8,128)(2,1)}, bf16[1024,256]{1,0:T(8,128)(2,1)}, u32[]{:S(2)}, u32[]{:S(2)}) %collective-permute-start.4) | collective-permute-done | bytes 524320 | tf_op jit(solution)/shard_map/ppermute | solution.py:18
  29.5 1.5 %collective-permute-start.5 = (bf16[1024,256]{1,0:T(8,128)(2,1)}, bf16[1024,256]{1,0:T(8,128)(2,1)}, u32[]{:S(2)}, u32[]{:S(2)}) collective-permute-start(bf16[1024,256]{1,0:T(8,128)(2,1)} %collective-permute-done.4), channel_id=1, source_target_pairs={{1,2},{2,1},{5,6},{6,5},{9,10},{10,9},{13,14},{14,13},{17,18},{18,... | collective-permute-start | bytes 1572872 | tf_op jit(solution)/shard_map/ppermute | solution.py:77
  31.1 2.1 %select_select_fusion.4 = bf16[1024,256]{1,0:T(8,128)(2,1)} fusion(bf16[1024,256]{1,0:T(8,128)(2,1)} %collective-permute-done.2, pred[]{:T(512)} %bitcast.8, pred[]{:T(512)S(6)} %or.3, bf16[1,1,1024,256]{3,2,1,0:T(8,128)(2,1)S(1)} %copy-done.2, bf16[256,256]{1,0:T(8,128)(2,1)S(1)} %get-tuple-element.77, bf16[256,256]{1,0:T(8,128)(2,1)S(1)} %get-tuple-element.78, ...), kind=kLoop, calls=%fused_computation.44 | loop fusion | flops 2621440 | bytes 2097154 | tf_op jit(solution)/shard_map/jit(_where)/select_n | solution.py:83
  33.2 7.0 %collective-permute-start.3 = (bf16[1024,256]{1,0:T(8,128)(2,1)}, bf16[1024,256]{1,0:T(8,128)(2,1)S(1)}, u32[]{:S(2)}, u32[]{:S(2)}) collective-permute-start(bf16[1024,256]{1,0:T(8,128)(2,1)} %select_select_fusion.4), channel_id=1, source_target_pairs={{0,1},{1,0},{2,3},{3,2},{4,5},{5,4},{6,7},{7,6},{8,9},{9,8},{10,11... | collective-permute-start | bytes 1572872 | tf_op jit(solution)/shard_map/ppermute | solution.py:18
  40.2 1.5 %collective-permute-start.7 = (bf16[1024,256]{1,0:T(8,128)(2,1)}, bf16[1024,256]{1,0:T(8,128)(2,1)}, u32[]{:S(2)}, u32[]{:S(2)}) collective-permute-start(bf16[1024,256]{1,0:T(8,128)(2,1)} %get-tuple-element.41), channel_id=1, source_target_pairs={{1,2},{2,1},{5,6},{6,5},{9,10},{10,9},{13,14},{14,13},{17,18},{18,... | collective-permute-start | bytes 1572872 | tf_op jit(solution)/shard_map/ppermute | solution.py:85
  41.7 1.7 %select_select_fusion.3 = bf16[1024,256]{1,0:T(8,128)(2,1)S(1)} fusion(bf16[1024,256]{1,0:T(8,128)(2,1)} %collective-permute-done.5, bf16[1024,256]{1,0:T(8,128)(2,1)} %copy-done.3, pred[]{:T(512)} %bitcast.9, pred[]{:T(512)} %bitcast.8, pred[]{:T(512)S(6)} %or.3, bf16[256,256]{1,0:T(8,128)(2,1)} %copy-done.13, bf16[256,256]{1,0:T(8,128)(2,1)} %copy-done.14, ...), kind=kLoop, calls=%fused_computation.43 | loop fusion | flops 2883584 | bytes 2621443 | tf_op jit(solution)/shard_map/jit(_where)/select_n | solution.py:93
  43.3 7.8 %collective-permute-start.6 = (bf16[1024,256]{1,0:T(8,128)(2,1)S(1)}, bf16[1024,256]{1,0:T(8,128)(2,1)S(1)}, u32[]{:S(2)}, u32[]{:S(2)}) collective-permute-start(bf16[1024,256]{1,0:T(8,128)(2,1)S(1)} %select_select_fusion.3), channel_id=1, source_target_pairs={{0,1},{1,0},{2,3},{3,2},{4,5},{5,4},{6,7},{7,6},{8,9},{9,8},{10,11... | collective-permute-start | bytes 1572872 | tf_op jit(solution)/shard_map/ppermute | solution.py:18
  53.7 7.7 %collective-permute-done.6 = bf16[1024,256]{1,0:T(8,128)(2,1)S(1)} collective-permute-done((bf16[1024,256]{1,0:T(8,128)(2,1)S(1)}, bf16[1024,256]{1,0:T(8,128)(2,1)S(1)}, u32[]{:S(2)}, u32[]{:S(2)}) %collective-permute-start.6) | collective-permute-done | bytes 524320 | tf_op jit(solution)/shard_map/ppermute | solution.py:18
  63.6 1.8 %collective-permute-start.10 = (bf16[256,1024]{1,0:T(8,128)(2,1)S(1)}, bf16[256,1024]{1,0:T(8,128)(2,1)S(1)}, u32[]{:S(2)}, u32[]{:S(2)}) collective-permute-start(bf16[256,1024]{1,0:T(8,128)(2,1)S(1)} %convolution_convert_fusion.2), channel_id=1, source_target_pairs={{0,1},{1,0},{2,3},{3,2},{4,5},{5,4},{6,7},{7,6},{8,9},{9,8},{10,11... | collective-permute-start | bytes 1572872 | tf_op jit(solution)/shard_map/ppermute | solution.py:18
  67.6 10.5 %collective-permute-done.10 = bf16[256,1024]{1,0:T(8,128)(2,1)S(1)} collective-permute-done((bf16[256,1024]{1,0:T(8,128)(2,1)S(1)}, bf16[256,1024]{1,0:T(8,128)(2,1)S(1)}, u32[]{:S(2)}, u32[]{:S(2)}) %collective-permute-start.10) | collective-permute-done | bytes 524320 | tf_op jit(solution)/shard_map/ppermute | solution.py:18
  78.1 1.3 %fusion.2 = bf16[256,1024]{1,0:T(8,128)(2,1)} fusion(pred[]{:T(512)} %bitcast.13, pred[]{:T(512)} %bitcast.11, pred[]{:T(512)} %bitcast.15, bf16[256,1024]{1,0:T(8,128)(2,1)S(1)} %pad_maximum_fusion.2, bf16[256,1024]{1,0:T(8,128)(2,1)S(1)} %subtract_convert_fusion.1, pred[]{:T(512)} %bitcast.14, bf16[256,1024]{1,0:T(8,128)(2,1)S(1)} %collective-permute-done.10, ...), kind=kLoop, calls=%fused_computation.15 | loop fusion | flops 3407872 | bytes 2621446 | tf_op jit(solution)/shard_map/convert_element_type | solution.py:234
  79.4 4.9 %collective-permute-start.12 = (bf16[256,1024]{1,0:T(8,128)(2,1)}, bf16[256,1024]{1,0:T(8,128)(2,1)}, u32[]{:S(2)}, u32[]{:S(2)}) collective-permute-start(bf16[256,1024]{1,0:T(8,128)(2,1)} %fusion.2), channel_id=1, source_target_pairs={{0,2},{1,3},{2,0},{3,1},{4,6},{5,7},{6,4},{7,5},{8,10},{9,11},{10,... | collective-permute-start | bytes 1572872 | tf_op jit(solution)/shard_map/ppermute | solution.py:18
  84.3 4.3 %collective-permute-done.11 = bf16[1024,256]{1,0:T(8,128)(2,1)S(1)} collective-permute-done((bf16[1024,256]{1,0:T(8,128)(2,1)S(1)}, bf16[1024,256]{1,0:T(8,128)(2,1)S(1)}, u32[]{:S(2)}, u32[]{:S(2)}) %collective-permute-start.11) | collective-permute-done | bytes 524320 | tf_op jit(solution)/shard_map/ppermute | solution.py:119
  89.6 1.4 %add_convert_fusion = bf16[384,1024]{1,0:T(8,128)(2,1)} fusion(f32[384,1024]{1,0:T(8,128)S(1)} %fusion.21, bf16[1024,256]{1,0:T(8,128)(2,1)S(1)} %get-tuple-element.59, f32[384,256]{1,0:T(8,128)S(1)} %fusion.39, f32[384,256]{1,0:T(8,128)S(1)} %convolution_bitcast_fusion, f32[384,256]{1,0:T(8,128)S(1)} %fusion.38), kind=kOutput, calls=%fused_computation | convolution fusion | flops 203096064 | bytes 4063232 | tf_op jit(solution)/shard_map/dot_general | solution.py:258
  91.0 3.9 %all-to-all-start.1 = ((bf16[8,48,1024]{2,1,0:T(8,128)(2,1)}), bf16[8,48,1024]{2,1,0:T(8,128)(2,1)S(1)}, u32[]{:S(2)}, u32[]{:S(2)}) async-start(bf16[8,48,1024]{2,1,0:T(8,128)(2,1)} %bitcast.61), calls=%async_computation.1 | async-start | bytes 1572864 | tf_op jit(solution)/shard_map/all_to_all | solution.py:262
  94.9 2.4 %fusion.11 = f32[256,1024]{1,0:T(8,128)S(1)} fusion(bf16[256,1024]{1,0:T(8,128)(2,1)} %bitcast.62, bf16[1,1,256,1024]{3,2,1,0:T(8,128)(2,1)} %param.18, pred[]{:T(512)S(6)} %eq.129, pred[]{:T(512)S(6)} %eq.128, pred[]{:T(512)S(6)} %eq.127, bf16[256,1024]{1,0:T(8,128)(2,1)S(1)} %pad_maximum_fusion.2, bf16[256,1024]{1,0:T(8,128)(2,1)S(1)} %subtract_convert_fusion.1, ...), kind=kLoop, calls=%fused_computation.24 | loop fusion | flops 6029312 | bytes 4718598 | tf_op jit(solution)/shard_map/sub | solution.py:241
  97.3 8.8 %collective-permute-done.12 = bf16[256,1024]{1,0:T(8,128)(2,1)} collective-permute-done((bf16[256,1024]{1,0:T(8,128)(2,1)}, bf16[256,1024]{1,0:T(8,128)(2,1)}, u32[]{:S(2)}, u32[]{:S(2)}) %collective-permute-start.12) | collective-permute-done | bytes 524320 | tf_op jit(solution)/shard_map/ppermute | solution.py:18
  106.2 2.0 %fusion.12 = bf16[1,1,256,1024]{3,2,1,0:T(8,128)(2,1)} fusion(f32[256,1024]{1,0:T(8,128)S(1)} %fusion.11, bf16[256,1024]{1,0:T(8,128)(2,1)} %collective-permute-done.12), kind=kLoop, calls=%fused_computation.28 | loop fusion | flops 1048576 | bytes 2097152 | tf_op jit(solution)/shard_map/broadcast_in_dim | solution.py:266
  (78 shorter events, 14.9 us)
Async XLA Ops:
  0.6 62.4 %copy-start = (bf16[1,1,8,48,1024]{4,3,2,1,0:T(8,128)(2,1)S(1)}, bf16[1,1,8,48,1024]{4,3,2,1,0:T(8,128)(2,1)}, u32[]{:S(2)}) copy-start(bf16[1,1,8,48,1024]{4,3,2,1,0:T(8,128)(2,1)} %param.19) | copy-start | bytes 2359300
  0.6 17.9 %collective-permute-start = (bf16[1024,256]{1,0:T(8,128)(2,1)}, bf16[1024,256]{1,0:T(8,128)(2,1)S(1)}, u32[]{:S(2)}, u32[]{:S(2)}) collective-permute-start(bf16[1024,256]{1,0:T(8,128)(2,1)} %bitcast.63), channel_id=1, source_target_pairs={{0,1},{3,2},{4,5},{7,6},{8,9},{11,10},{12,13},{15,14},{16,17},{19,... | collective-permute-start | bytes 1572872 | tf_op jit(solution)/shard_map/ppermute | solution.py:63
  5.7 12.8 %collective-permute-start.1 = (bf16[1024,256]{1,0:T(8,128)(2,1)}, bf16[1024,256]{1,0:T(8,128)(2,1)S(1)}, u32[]{:S(2)}, u32[]{:S(2)}) collective-permute-start(bf16[1024,256]{1,0:T(8,128)(2,1)} %bitcast.64), channel_id=1, source_target_pairs={{1,2},{2,1},{5,6},{6,5},{9,10},{10,9},{13,14},{14,13},{17,18},{18,... | collective-permute-start | bytes 1572872 | tf_op jit(solution)/shard_map/ppermute | solution.py:64
  14.4 5.0 %copy-start.2 = (bf16[1,1,1024,256]{3,2,1,0:T(8,128)(2,1)S(1)}, bf16[1,1,1024,256]{3,2,1,0:T(8,128)(2,1)}, u32[]{:S(2)}) copy-start(bf16[1,1,1024,256]{3,2,1,0:T(8,128)(2,1)} %param.15) | copy-start | bytes 1572868
  15.4 14.1 %collective-permute-start.4 = (bf16[1024,256]{1,0:T(8,128)(2,1)}, bf16[1024,256]{1,0:T(8,128)(2,1)}, u32[]{:S(2)}, u32[]{:S(2)}) collective-permute-start(bf16[1024,256]{1,0:T(8,128)(2,1)} %broadcast_select_fusion.3), channel_id=1, source_target_pairs={{0,1},{1,0},{2,3},{3,2},{4,5},{5,4},{6,7},{7,6},{8,9},{9,8},{10,11... | collective-permute-start | bytes 1572872 | tf_op jit(solution)/shard_map/ppermute | solution.py:18
  20.5 10.6 %copy-start.1 = (bf16[1,1,256,1024]{3,2,1,0:T(8,128)(2,1)S(1)}, bf16[1,1,256,1024]{3,2,1,0:T(8,128)(2,1)}, u32[]{:S(2)}) copy-start(bf16[1,1,256,1024]{3,2,1,0:T(8,128)(2,1)} %param.16) | copy-start | bytes 1572868
  20.5 10.6 %collective-permute-start.2 = (bf16[1024,256]{1,0:T(8,128)(2,1)}, bf16[1024,256]{1,0:T(8,128)(2,1)}, u32[]{:S(2)}, u32[]{:S(2)}) collective-permute-start(bf16[1024,256]{1,0:T(8,128)(2,1)} %get-tuple-element.63), channel_id=1, source_target_pairs={{1,2},{2,1},{5,6},{6,5},{9,10},{10,9},{13,14},{14,13},{17,18},{18,... | collective-permute-start | bytes 1572872 | tf_op jit(solution)/shard_map/ppermute | solution.py:75
  23.4 18.2 %all-to-all-start = ((bf16[8,48,1024]{2,1,0:T(8,128)(2,1)}), bf16[8,48,1024]{2,1,0:T(8,128)(2,1)S(1)}, u32[]{:S(2)}, u32[]{:S(2)}) async-start(bf16[8,48,1024]{2,1,0:T(8,128)(2,1)} %bitcast.17), calls=%async_computation | async-start | bytes 1572864 | tf_op jit(solution)/shard_map/all_to_all | solution.py:180
  29.5 12.1 %collective-permute-start.5 = (bf16[1024,256]{1,0:T(8,128)(2,1)}, bf16[1024,256]{1,0:T(8,128)(2,1)}, u32[]{:S(2)}, u32[]{:S(2)}) collective-permute-start(bf16[1024,256]{1,0:T(8,128)(2,1)} %collective-permute-done.4), channel_id=1, source_target_pairs={{1,2},{2,1},{5,6},{6,5},{9,10},{10,9},{13,14},{14,13},{17,18},{18,... | collective-permute-start | bytes 1572872 | tf_op jit(solution)/shard_map/ppermute | solution.py:77
  31.1 10.6 %copy-start.10 = (bf16[256,256]{1,0:T(8,128)(2,1)}, bf16[256,256]{1,0:T(8,128)(2,1)S(1)}, u32[]{:S(2)}) copy-start(bf16[256,256]{1,0:T(8,128)(2,1)S(1)} %get-tuple-element.79) | copy-start | bytes 393220
  33.2 18.0 %collective-permute-start.3 = (bf16[1024,256]{1,0:T(8,128)(2,1)}, bf16[1024,256]{1,0:T(8,128)(2,1)S(1)}, u32[]{:S(2)}, u32[]{:S(2)}) collective-permute-start(bf16[1024,256]{1,0:T(8,128)(2,1)} %select_select_fusion.4), channel_id=1, source_target_pairs={{0,1},{1,0},{2,3},{3,2},{4,5},{5,4},{6,7},{7,6},{8,9},{9,8},{10,11... | collective-permute-start | bytes 1572872 | tf_op jit(solution)/shard_map/ppermute | solution.py:18
  40.2 12.0 %collective-permute-start.7 = (bf16[1024,256]{1,0:T(8,128)(2,1)}, bf16[1024,256]{1,0:T(8,128)(2,1)}, u32[]{:S(2)}, u32[]{:S(2)}) collective-permute-start(bf16[1024,256]{1,0:T(8,128)(2,1)} %get-tuple-element.41), channel_id=1, source_target_pairs={{1,2},{2,1},{5,6},{6,5},{9,10},{10,9},{13,14},{14,13},{17,18},{18,... | collective-permute-start | bytes 1572872 | tf_op jit(solution)/shard_map/ppermute | solution.py:85
  41.7 9.5 %copy-start.11 = (bf16[256,256]{1,0:T(8,128)(2,1)S(1)}, bf16[256,256]{1,0:T(8,128)(2,1)}, u32[]{:S(2)}) copy-start(bf16[256,256]{1,0:T(8,128)(2,1)} %copy-done.10) | copy-start | bytes 393220
  43.3 8.8 %copy-start.6 = (bf16[1024,256]{1,0:T(8,128)(2,1)S(1)}, bf16[1024,256]{1,0:T(8,128)(2,1)}, u32[]{:S(2)}) copy-start(bf16[1024,256]{1,0:T(8,128)(2,1)} %copy-done.5) | copy-start | bytes 1572868
  43.3 18.1 %collective-permute-start.6 = (bf16[1024,256]{1,0:T(8,128)(2,1)S(1)}, bf16[1024,256]{1,0:T(8,128)(2,1)S(1)}, u32[]{:S(2)}, u32[]{:S(2)}) collective-permute-start(bf16[1024,256]{1,0:T(8,128)(2,1)S(1)} %select_select_fusion.3), channel_id=1, source_target_pairs={{0,1},{1,0},{2,3},{3,2},{4,5},{5,4},{6,7},{7,6},{8,9},{9,8},{10,11... | collective-permute-start | bytes 1572872 | tf_op jit(solution)/shard_map/ppermute | solution.py:18
  51.3 10.1 %copy-start.4 = (bf16[1024,256]{1,0:T(8,128)(2,1)S(1)}, bf16[1024,256]{1,0:T(8,128)(2,1)}, u32[]{:S(2)}) copy-start(bf16[1024,256]{1,0:T(8,128)(2,1)} %copy-done.3) | copy-start | bytes 1572868
  51.3 14.7 %collective-permute-start.9 = (bf16[1024,256]{1,0:T(8,128)(2,1)S(1)}, bf16[1024,256]{1,0:T(8,128)(2,1)S(1)}, u32[]{:S(2)}, u32[]{:S(2)}) collective-permute-start(bf16[1024,256]{1,0:T(8,128)(2,1)S(1)} %get-tuple-element.61), channel_id=1, source_target_pairs={{1,2},{2,1},{5,6},{6,5},{9,10},{10,9},{13,14},{14,13},{17,18},{18,... | collective-permute-start | bytes 1572872 | tf_op jit(solution)/shard_map/ppermute | solution.py:98
  63.6 25.2 %copy-start.7 = (bf16[256,1024]{1,0:T(8,128)(2,1)}, bf16[256,1024]{1,0:T(8,128)(2,1)S(1)}, u32[]{:S(2)}) copy-start(bf16[256,1024]{1,0:T(8,128)(2,1)S(1)} %convolution_convert_fusion.2) | copy-start | bytes 1572868
  63.6 14.5 %collective-permute-start.10 = (bf16[256,1024]{1,0:T(8,128)(2,1)S(1)}, bf16[256,1024]{1,0:T(8,128)(2,1)S(1)}, u32[]{:S(2)}, u32[]{:S(2)}) collective-permute-start(bf16[256,1024]{1,0:T(8,128)(2,1)S(1)} %convolution_convert_fusion.2), channel_id=1, source_target_pairs={{0,1},{1,0},{2,3},{3,2},{4,5},{5,4},{6,7},{7,6},{8,9},{9,8},{10,11... | collective-permute-start | bytes 1572872 | tf_op jit(solution)/shard_map/ppermute | solution.py:18
  65.4 2.3 %collective-permute-start.8 = (bf16[1024,256]{1,0:T(8,128)(2,1)S(1)}, bf16[1024,256]{1,0:T(8,128)(2,1)S(1)}, u32[]{:S(2)}, u32[]{:S(2)}) collective-permute-start(bf16[1024,256]{1,0:T(8,128)(2,1)S(1)} %get-tuple-element.45), channel_id=1, source_target_pairs={{1,2},{2,1},{5,6},{6,5},{9,10},{10,9},{13,14},{14,13},{17,18},{18,... | collective-permute-start | bytes 1572872 | tf_op jit(solution)/shard_map/ppermute | solution.py:115
  66.2 22.4 %collective-permute-start.11 = (bf16[1024,256]{1,0:T(8,128)(2,1)S(1)}, bf16[1024,256]{1,0:T(8,128)(2,1)S(1)}, u32[]{:S(2)}, u32[]{:S(2)}) collective-permute-start(bf16[1024,256]{1,0:T(8,128)(2,1)S(1)} %broadcast_select_fusion.8), channel_id=1, source_target_pairs={{1,0},{2,3},{5,4},{6,7},{9,8},{10,11},{13,12},{14,15},{17,16},{18,... | collective-permute-start | bytes 1572872 | tf_op jit(solution)/shard_map/ppermute | solution.py:119
  78.1 10.6 %copy-start.8 = (bf16[256,1024]{1,0:T(8,128)(2,1)}, bf16[256,1024]{1,0:T(8,128)(2,1)S(1)}, u32[]{:S(2)}) copy-start(bf16[256,1024]{1,0:T(8,128)(2,1)S(1)} %collective-permute-done.10) | copy-start | bytes 1572868
  79.4 26.8 %collective-permute-start.12 = (bf16[256,1024]{1,0:T(8,128)(2,1)}, bf16[256,1024]{1,0:T(8,128)(2,1)}, u32[]{:S(2)}, u32[]{:S(2)}) collective-permute-start(bf16[256,1024]{1,0:T(8,128)(2,1)} %fusion.2), channel_id=1, source_target_pairs={{0,2},{1,3},{2,0},{3,1},{4,6},{5,7},{6,4},{7,5},{8,10},{9,11},{10,... | collective-permute-start | bytes 1572872 | tf_op jit(solution)/shard_map/ppermute | solution.py:18
  91.0 17.2 %all-to-all-start.1 = ((bf16[8,48,1024]{2,1,0:T(8,128)(2,1)}), bf16[8,48,1024]{2,1,0:T(8,128)(2,1)S(1)}, u32[]{:S(2)}, u32[]{:S(2)}) async-start(bf16[8,48,1024]{2,1,0:T(8,128)(2,1)} %bitcast.61), calls=%async_computation.1 | async-start | bytes 1572864 | tf_op jit(solution)/shard_map/all_to_all | solution.py:262
  (9 other events, 25.6 us)
where the time goes:
time: 110 us; the launch traced here: 109 us
  starting transfers between devices  44.4 us (40%)
  waiting for transfers between devices  33.8 us (31%)
  other arithmetic  17.2 us (16%)
  between operations  6.2 us (6%)
  matrix products  6.12 us (6%)
  local copies, waits for them, and re-layouts  1.81 us (2%)
    ppermute x5, waiting for transfers between devices, from_partner(): return lax.ppermute(value, 'rep', pairs)  29.4 us
    ppermute x5, starting transfers between devices, from_partner(): return lax.ppermute(value, 'rep', pairs)  23.6 us
    ppermute x1, starting transfers between devices, forward(): self.up_side = lax.ppermute(self.up, 'rep', INWARD)  5.09 us
    ppermute x1, waiting for transfers between devices, handed_down(): self.four = lax.ppermute(send, 'rep', OUTWARD)  4.34 us
    all_to_all x1, starting transfers between devices, on_device(): lax.all_to_all(slot_grad, 'section', split_axis=0, concat_axis=0, tiled=T...  3.94 us
    all_to_all x1, starting transfers between devices, on_device(): lax.all_to_all(dispatched, 'section', split_axis=0, concat_axis=0, tiled=...  3.72 us
    sub x1, other arithmetic, on_device(): slow_float - pull * outer_here  2.38 us
  transfers between devices with their start and end apart: 15, of which 5 were waited for; matrix products, arithmetic and copies ran while one was open for 21% of the time, Pallas kernels for 0%

commit v1 on v0

--- a/solution.py
+++ b/solution.py
@@ -190,6 +190,7 @@
 
     up_act = jnp.dot(rows, up_mat, preferred_element_type=jnp.float32)
     if line is not None:
+        line.swap_down((up_act,))
         gate_mat, static_in = line.gate_here((up_act,))
         static_in = side_by_side(static_in)
     gate_act = jnp.dot(rows, gate_mat, preferred_element_type=jnp.float32)
@@ -198,9 +199,6 @@
     down_grad = lax.dot_general(
         hidden, cotangent, (((0,), (0,)), ((), ())), preferred_element_type=jnp.float32
     ).astype(jnp.bfloat16)
-
-    if line is not None:
-        line.swap_down((down_grad,))
 
     own_bits, mine_bits, match_bits = [
         bits[number * levels : (number + 1) * levels] for number in range(3)

time: 110 us -> 111 us (level)
    ppermute x5, waiting for transfers between devices: 29.4 us -> 27.4 us  [from_partner(): return lax.ppermute(value, 'rep', pairs)]
    ppermute x1, waiting for transfers between devices: 4.34 us -> 5.97 us  [handed_down(): self.four = lax.ppermute(send, 'rep', OUTWARD)]
  transfers between devices with their start and end apart: 15 -> 15, of which waited for: 5 -> 6; matrix products, arithmetic and copies ran while one was open for 21% -> 21% of each run, Pallas kernels for 0% -> 0%
where the time goes in v1:
time: 111 us
  starting transfers between devices  44.6 us (40%)
  waiting for transfers between devices  34.4 us (31%)
  other arithmetic  17.3 us (16%)
  between operations  6.2 us (6%)
  matrix products  6.13 us (6%)
  local copies, waits for them, and re-layouts  1.81 us (2%)
    ppermute x5, waiting for transfers between devices, from_partner(): return lax.ppermute(value, 'rep', pairs)  27.4 us
    ppermute x5, starting transfers between devices, from_partner(): return lax.ppermute(value, 'rep', pairs)  23.8 us
    ppermute x1, waiting for transfers between devices, handed_down(): self.four = lax.ppermute(send, 'rep', OUTWARD)  5.97 us
    ppermute x1, starting transfers between devices, forward(): self.up_side = lax.ppermute(self.up, 'rep', INWARD)  5.09 us
    all_to_all x1, starting transfers between devices, on_device(): lax.all_to_all(slot_grad, 'section', split_axis=0, concat_axis=0, tiled=T...  3.99 us
    all_to_all x1, starting transfers between devices, on_device(): lax.all_to_all(dispatched, 'section', split_axis=0, concat_axis=0, tiled=...  3.72 us
    sub x1, other arithmetic, on_device(): slow_float - pull * outer_here  2.38 us
  transfers between devices with their start and end apart: 15, of which 6 were waited for; matrix products, arithmetic and copies ran while one was open for 21% of the time, Pallas kernels for 0%

profile of v1, /device:TPU:0, one launch (start us, length us, event | category | flops | bytes accessed | tf_op | source)
XLA Modules:
  0.0 110.5 jit_solution(15444839401348010605)
XLA Ops:
  0.6 5.1 %collective-permute-start = (bf16[1024,256]{1,0:T(8,128)(2,1)}, bf16[1024,256]{1,0:T(8,128)(2,1)S(1)}, u32[]{:S(2)}, u32[]{:S(2)}) collective-permute-start(bf16[1024,256]{1,0:T(8,128)(2,1)} %bitcast.63), channel_id=1, source_target_pairs={{0,1},{3,2},{4,5},{7,6},{8,9},{11,10},{12,13},{15,14},{16,17},{19,... | collective-permute-start | bytes 1572872 | tf_op jit(solution)/shard_map/ppermute | solution.py:63
  12.9 1.4 %subtract_convert_fusion.1 = bf16[256,1024]{1,0:T(8,128)(2,1)S(1)} fusion(bf16[1,1,256,1024]{3,2,1,0:T(8,128)(2,1)} %param.17, bf16[1,1,256,1024]{3,2,1,0:T(8,128)(2,1)} %param.16), kind=kLoop, calls=%fused_computation.26 | loop fusion | flops 1572864 | bytes 1572864 | tf_op jit(solution)/shard_map/convert_element_type | solution.py:160
  15.4 2.1 %collective-permute-start.4 = (bf16[1024,256]{1,0:T(8,128)(2,1)}, bf16[1024,256]{1,0:T(8,128)(2,1)}, u32[]{:S(2)}, u32[]{:S(2)}) collective-permute-start(bf16[1024,256]{1,0:T(8,128)(2,1)} %broadcast_select_fusion.3), channel_id=1, source_target_pairs={{0,1},{1,0},{2,3},{3,2},{4,5},{5,4},{6,7},{7,6},{8,9},{9,8},{10,11... | collective-permute-start | bytes 1572872 | tf_op jit(solution)/shard_map/ppermute | solution.py:18
  20.5 1.6 %collective-permute-start.2 = (bf16[1024,256]{1,0:T(8,128)(2,1)}, bf16[1024,256]{1,0:T(8,128)(2,1)}, u32[]{:S(2)}, u32[]{:S(2)}) collective-permute-start(bf16[1024,256]{1,0:T(8,128)(2,1)} %get-tuple-element.63), channel_id=1, source_target_pairs={{1,2},{2,1},{5,6},{6,5},{9,10},{10,9},{13,14},{14,13},{17,18},{18,... | collective-permute-start | bytes 1572872 | tf_op jit(solution)/shard_map/ppermute | solution.py:75
  22.1 1.4 %convolution_convert_fusion = bf16[384,1024]{1,0:T(8,128)(2,1)} fusion(bf16[1,1,256,1024]{3,2,1,0:T(8,128)(2,1)S(1)} %copy-done.16, s32[256]{0:T(256)S(1)} %multiply_add_fusion), kind=kOutput, calls=%fused_computation.1 | convolution fusion | flops 201818112 | bytes 1311744 | tf_op jit(solution)/shard_map/dot_general | solution.py:163
  23.4 3.7 %all-to-all-start = ((bf16[8,48,1024]{2,1,0:T(8,128)(2,1)}), bf16[8,48,1024]{2,1,0:T(8,128)(2,1)S(1)}, u32[]{:S(2)}, u32[]{:S(2)}) async-start(bf16[8,48,1024]{2,1,0:T(8,128)(2,1)} %bitcast.17), calls=%async_computation | async-start | bytes 1572864 | tf_op jit(solution)/shard_map/all_to_all | solution.py:180
  27.2 2.4 %collective-permute-done.4 = bf16[1024,256]{1,0:T(8,128)(2,1)} collective-permute-done((bf16[1024,256]{1,0:T(8,128)(2,1)}, bf16[1024,256]{1,0:T(8,128)(2,1)}, u32[]{:S(2)}, u32[]{:S(2)}) %collective-permute-start.4) | collective-permute-done | bytes 524320 | tf_op jit(solution)/shard_map/ppermute | solution.py:18
  29.5 1.5 %collective-permute-start.5 = (bf16[1024,256]{1,0:T(8,128)(2,1)}, bf16[1024,256]{1,0:T(8,128)(2,1)}, u32[]{:S(2)}, u32[]{:S(2)}) collective-permute-start(bf16[1024,256]{1,0:T(8,128)(2,1)} %collective-permute-done.4), channel_id=1, source_target_pairs={{1,2},{2,1},{5,6},{6,5},{9,10},{10,9},{13,14},{14,13},{17,18},{18,... | collective-permute-start | bytes 1572872 | tf_op jit(solution)/shard_map/ppermute | solution.py:77
  31.1 2.1 %select_select_fusion.4 = bf16[1024,256]{1,0:T(8,128)(2,1)} fusion(bf16[1024,256]{1,0:T(8,128)(2,1)} %collective-permute-done.2, pred[]{:T(512)} %bitcast.8, pred[]{:T(512)S(6)} %or.3, bf16[1,1,1024,256]{3,2,1,0:T(8,128)(2,1)S(1)} %copy-done.2, bf16[256,256]{1,0:T(8,128)(2,1)S(1)} %get-tuple-element.77, bf16[256,256]{1,0:T(8,128)(2,1)S(1)} %get-tuple-element.78, ...), kind=kLoop, calls=%fused_computation.44 | loop fusion | flops 2621440 | bytes 2097154 | tf_op jit(solution)/shard_map/jit(_where)/select_n | solution.py:83
  33.2 7.0 %collective-permute-start.3 = (bf16[1024,256]{1,0:T(8,128)(2,1)}, bf16[1024,256]{1,0:T(8,128)(2,1)S(1)}, u32[]{:S(2)}, u32[]{:S(2)}) collective-permute-start(bf16[1024,256]{1,0:T(8,128)(2,1)} %select_select_fusion.4), channel_id=1, source_target_pairs={{0,1},{1,0},{2,3},{3,2},{4,5},{5,4},{6,7},{7,6},{8,9},{9,8},{10,11... | collective-permute-start | bytes 1572872 | tf_op jit(solution)/shard_map/ppermute | solution.py:18
  40.2 1.5 %collective-permute-start.6 = (bf16[1024,256]{1,0:T(8,128)(2,1)}, bf16[1024,256]{1,0:T(8,128)(2,1)}, u32[]{:S(2)}, u32[]{:S(2)}) collective-permute-start(bf16[1024,256]{1,0:T(8,128)(2,1)} %get-tuple-element.41), channel_id=1, source_target_pairs={{1,2},{2,1},{5,6},{6,5},{9,10},{10,9},{13,14},{14,13},{17,18},{18,... | collective-permute-start | bytes 1572872 | tf_op jit(solution)/shard_map/ppermute | solution.py:85
  41.7 1.7 %select_select_fusion.3 = bf16[1024,256]{1,0:T(8,128)(2,1)S(1)} fusion(bf16[1024,256]{1,0:T(8,128)(2,1)} %collective-permute-done.5, bf16[1024,256]{1,0:T(8,128)(2,1)} %copy-done.3, pred[]{:T(512)} %bitcast.9, pred[]{:T(512)} %bitcast.8, pred[]{:T(512)S(6)} %or.3, bf16[256,256]{1,0:T(8,128)(2,1)} %copy-done.13, bf16[256,256]{1,0:T(8,128)(2,1)} %copy-done.14, ...), kind=kLoop, calls=%fused_computation.43 | loop fusion | flops 2883584 | bytes 2621443 | tf_op jit(solution)/shard_map/jit(_where)/select_n | solution.py:93
  43.3 7.8 %collective-permute-start.8 = (bf16[1024,256]{1,0:T(8,128)(2,1)S(1)}, bf16[1024,256]{1,0:T(8,128)(2,1)S(1)}, u32[]{:S(2)}, u32[]{:S(2)}) collective-permute-start(bf16[1024,256]{1,0:T(8,128)(2,1)S(1)} %select_select_fusion.3), channel_id=1, source_target_pairs={{0,1},{1,0},{2,3},{3,2},{4,5},{5,4},{6,7},{7,6},{8,9},{9,8},{10,11... | collective-permute-start | bytes 1572872 | tf_op jit(solution)/shard_map/ppermute | solution.py:18
  54.4 7.0 %collective-permute-done.8 = bf16[1024,256]{1,0:T(8,128)(2,1)S(1)} collective-permute-done((bf16[1024,256]{1,0:T(8,128)(2,1)S(1)}, bf16[1024,256]{1,0:T(8,128)(2,1)S(1)}, u32[]{:S(2)}, u32[]{:S(2)}) %collective-permute-start.8) | collective-permute-done | bytes 524320 | tf_op jit(solution)/shard_map/ppermute | solution.py:18
  61.5 1.3 %broadcast_select_fusion.9 = (bf16[1024,256]{1,0:T(8,128)(2,1)S(1)}, bf16[1024,256]{1,0:T(8,128)(2,1)S(1)}) fusion(bf16[1024,256]{1,0:T(8,128)(2,1)S(1)} %collective-permute-done.8, bf16[1024,256]{1,0:T(8,128)(2,1)} %collective-permute-done.4, pred[]{:T(512)S(6)} %or.3, bf16[1024,256]{1,0:T(8,128)(2,1)S(1)} %copy-done.4, ...), kind=kLoop, calls=%fused_computation.54 | loop fusion | flops 1048576 | bytes 3145731 | tf_op jit(solution)/shard_map/jit(_where)/select_n | solution.py:110
  63.7 5.2 %collective-permute-start.10 = (bf16[256,1024]{1,0:T(8,128)(2,1)S(1)}, bf16[256,1024]{1,0:T(8,128)(2,1)S(1)}, u32[]{:S(2)}, u32[]{:S(2)}) collective-permute-start(bf16[256,1024]{1,0:T(8,128)(2,1)S(1)} %convolution_convert_fusion.2), channel_id=1, source_target_pairs={{0,1},{1,0},{2,3},{3,2},{4,5},{5,4},{6,7},{7,6},{8,9},{9,8},{10,11... | collective-permute-start | bytes 1572872 | tf_op jit(solution)/shard_map/ppermute | solution.py:18
  70.5 10.9 %collective-permute-done.10 = bf16[256,1024]{1,0:T(8,128)(2,1)S(1)} collective-permute-done((bf16[256,1024]{1,0:T(8,128)(2,1)S(1)}, bf16[256,1024]{1,0:T(8,128)(2,1)S(1)}, u32[]{:S(2)}, u32[]{:S(2)}) %collective-permute-start.10) | collective-permute-done | bytes 524320 | tf_op jit(solution)/shard_map/ppermute | solution.py:18
  82.7 1.6 %collective-permute-start.12 = (bf16[256,1024]{1,0:T(8,128)(2,1)}, bf16[256,1024]{1,0:T(8,128)(2,1)}, u32[]{:S(2)}, u32[]{:S(2)}) collective-permute-start(bf16[256,1024]{1,0:T(8,128)(2,1)} %fusion.2), channel_id=1, source_target_pairs={{0,2},{1,3},{2,0},{3,1},{4,6},{5,7},{6,4},{7,5},{8,10},{9,11},{10,... | collective-permute-start | bytes 1572872 | tf_op jit(solution)/shard_map/ppermute | solution.py:18
  84.3 6.0 %collective-permute-done.11 = bf16[1024,256]{1,0:T(8,128)(2,1)S(1)} collective-permute-done((bf16[1024,256]{1,0:T(8,128)(2,1)S(1)}, bf16[1024,256]{1,0:T(8,128)(2,1)S(1)}, u32[]{:S(2)}, u32[]{:S(2)}) %collective-permute-start.11) | collective-permute-done | bytes 524320 | tf_op jit(solution)/shard_map/ppermute | solution.py:119
  91.2 1.4 %add_convert_fusion = bf16[384,1024]{1,0:T(8,128)(2,1)} fusion(f32[384,1024]{1,0:T(8,128)S(1)} %fusion.21, bf16[1024,256]{1,0:T(8,128)(2,1)S(1)} %get-tuple-element.59, f32[384,256]{1,0:T(8,128)S(1)} %fusion.39, f32[384,256]{1,0:T(8,128)S(1)} %convolution_bitcast_fusion, f32[384,256]{1,0:T(8,128)S(1)} %fusion.38), kind=kOutput, calls=%fused_computation | convolution fusion | flops 203096064 | bytes 4063232 | tf_op jit(solution)/shard_map/dot_general | solution.py:256
  92.6 4.0 %all-to-all-start.1 = ((bf16[8,48,1024]{2,1,0:T(8,128)(2,1)}), bf16[8,48,1024]{2,1,0:T(8,128)(2,1)S(1)}, u32[]{:S(2)}, u32[]{:S(2)}) async-start(bf16[8,48,1024]{2,1,0:T(8,128)(2,1)} %bitcast.61), calls=%async_computation.1 | async-start | bytes 1572864 | tf_op jit(solution)/shard_map/all_to_all | solution.py:260
  96.6 2.4 %fusion.11 = f32[256,1024]{1,0:T(8,128)S(1)} fusion(bf16[256,1024]{1,0:T(8,128)(2,1)} %bitcast.62, bf16[1,1,256,1024]{3,2,1,0:T(8,128)(2,1)} %param.18, pred[]{:T(512)S(6)} %eq.129, pred[]{:T(512)S(6)} %eq.128, pred[]{:T(512)S(6)} %eq.127, bf16[256,1024]{1,0:T(8,128)(2,1)S(1)} %pad_maximum_fusion.2, bf16[256,1024]{1,0:T(8,128)(2,1)S(1)} %subtract_convert_fusion.1, ...), kind=kLoop, calls=%fused_computation.24 | loop fusion | flops 6029312 | bytes 4718598 | tf_op jit(solution)/shard_map/sub | solution.py:239
  99.0 7.2 %collective-permute-done.12 = bf16[256,1024]{1,0:T(8,128)(2,1)} collective-permute-done((bf16[256,1024]{1,0:T(8,128)(2,1)}, bf16[256,1024]{1,0:T(8,128)(2,1)}, u32[]{:S(2)}, u32[]{:S(2)}) %collective-permute-start.12) | collective-permute-done | bytes 524320 | tf_op jit(solution)/shard_map/ppermute | solution.py:18
  106.2 2.0 %fusion.12 = bf16[1,1,256,1024]{3,2,1,0:T(8,128)(2,1)} fusion(f32[256,1024]{1,0:T(8,128)S(1)} %fusion.11, bf16[256,1024]{1,0:T(8,128)(2,1)} %collective-permute-done.12), kind=kLoop, calls=%fused_computation.28 | loop fusion | flops 1048576 | bytes 2097152 | tf_op jit(solution)/shard_map/broadcast_in_dim | solution.py:264
  (78 shorter events, 16.1 us)
Async XLA Ops:
  0.6 62.5 %copy-start = (bf16[1,1,8,48,1024]{4,3,2,1,0:T(8,128)(2,1)S(1)}, bf16[1,1,8,48,1024]{4,3,2,1,0:T(8,128)(2,1)}, u32[]{:S(2)}) copy-start(bf16[1,1,8,48,1024]{4,3,2,1,0:T(8,128)(2,1)} %param.19) | copy-start | bytes 2359300
  0.6 17.9 %collective-permute-start = (bf16[1024,256]{1,0:T(8,128)(2,1)}, bf16[1024,256]{1,0:T(8,128)(2,1)S(1)}, u32[]{:S(2)}, u32[]{:S(2)}) collective-permute-start(bf16[1024,256]{1,0:T(8,128)(2,1)} %bitcast.63), channel_id=1, source_target_pairs={{0,1},{3,2},{4,5},{7,6},{8,9},{11,10},{12,13},{15,14},{16,17},{19,... | collective-permute-start | bytes 1572872 | tf_op jit(solution)/shard_map/ppermute | solution.py:63
  5.7 12.8 %collective-permute-start.1 = (bf16[1024,256]{1,0:T(8,128)(2,1)}, bf16[1024,256]{1,0:T(8,128)(2,1)S(1)}, u32[]{:S(2)}, u32[]{:S(2)}) collective-permute-start(bf16[1024,256]{1,0:T(8,128)(2,1)} %bitcast.64), channel_id=1, source_target_pairs={{1,2},{2,1},{5,6},{6,5},{9,10},{10,9},{13,14},{14,13},{17,18},{18,... | collective-permute-start | bytes 1572872 | tf_op jit(solution)/shard_map/ppermute | solution.py:64
  14.4 5.0 %copy-start.2 = (bf16[1,1,1024,256]{3,2,1,0:T(8,128)(2,1)S(1)}, bf16[1,1,1024,256]{3,2,1,0:T(8,128)(2,1)}, u32[]{:S(2)}) copy-start(bf16[1,1,1024,256]{3,2,1,0:T(8,128)(2,1)} %param.15) | copy-start | bytes 1572868
  15.4 14.1 %collective-permute-start.4 = (bf16[1024,256]{1,0:T(8,128)(2,1)}, bf16[1024,256]{1,0:T(8,128)(2,1)}, u32[]{:S(2)}, u32[]{:S(2)}) collective-permute-start(bf16[1024,256]{1,0:T(8,128)(2,1)} %broadcast_select_fusion.3), channel_id=1, source_target_pairs={{0,1},{1,0},{2,3},{3,2},{4,5},{5,4},{6,7},{7,6},{8,9},{9,8},{10,11... | collective-permute-start | bytes 1572872 | tf_op jit(solution)/shard_map/ppermute | solution.py:18
  20.5 10.6 %copy-start.1 = (bf16[1,1,256,1024]{3,2,1,0:T(8,128)(2,1)S(1)}, bf16[1,1,256,1024]{3,2,1,0:T(8,128)(2,1)}, u32[]{:S(2)}) copy-start(bf16[1,1,256,1024]{3,2,1,0:T(8,128)(2,1)} %param.16) | copy-start | bytes 1572868
  20.5 10.6 %collective-permute-start.2 = (bf16[1024,256]{1,0:T(8,128)(2,1)}, bf16[1024,256]{1,0:T(8,128)(2,1)}, u32[]{:S(2)}, u32[]{:S(2)}) collective-permute-start(bf16[1024,256]{1,0:T(8,128)(2,1)} %get-tuple-element.63), channel_id=1, source_target_pairs={{1,2},{2,1},{5,6},{6,5},{9,10},{10,9},{13,14},{14,13},{17,18},{18,... | collective-permute-start | bytes 1572872 | tf_op jit(solution)/shard_map/ppermute | solution.py:75
  23.4 18.2 %all-to-all-start = ((bf16[8,48,1024]{2,1,0:T(8,128)(2,1)}), bf16[8,48,1024]{2,1,0:T(8,128)(2,1)S(1)}, u32[]{:S(2)}, u32[]{:S(2)}) async-start(bf16[8,48,1024]{2,1,0:T(8,128)(2,1)} %bitcast.17), calls=%async_computation | async-start | bytes 1572864 | tf_op jit(solution)/shard_map/all_to_all | solution.py:180
  29.5 12.1 %collective-permute-start.5 = (bf16[1024,256]{1,0:T(8,128)(2,1)}, bf16[1024,256]{1,0:T(8,128)(2,1)}, u32[]{:S(2)}, u32[]{:S(2)}) collective-permute-start(bf16[1024,256]{1,0:T(8,128)(2,1)} %collective-permute-done.4), channel_id=1, source_target_pairs={{1,2},{2,1},{5,6},{6,5},{9,10},{10,9},{13,14},{14,13},{17,18},{18,... | collective-permute-start | bytes 1572872 | tf_op jit(solution)/shard_map/ppermute | solution.py:77
  31.1 10.6 %copy-start.10 = (bf16[256,256]{1,0:T(8,128)(2,1)}, bf16[256,256]{1,0:T(8,128)(2,1)S(1)}, u32[]{:S(2)}) copy-start(bf16[256,256]{1,0:T(8,128)(2,1)S(1)} %get-tuple-element.79) | copy-start | bytes 393220
  33.2 18.0 %collective-permute-start.3 = (bf16[1024,256]{1,0:T(8,128)(2,1)}, bf16[1024,256]{1,0:T(8,128)(2,1)S(1)}, u32[]{:S(2)}, u32[]{:S(2)}) collective-permute-start(bf16[1024,256]{1,0:T(8,128)(2,1)} %select_select_fusion.4), channel_id=1, source_target_pairs={{0,1},{1,0},{2,3},{3,2},{4,5},{5,4},{6,7},{7,6},{8,9},{9,8},{10,11... | collective-permute-start | bytes 1572872 | tf_op jit(solution)/shard_map/ppermute | solution.py:18
  40.2 12.0 %collective-permute-start.6 = (bf16[1024,256]{1,0:T(8,128)(2,1)}, bf16[1024,256]{1,0:T(8,128)(2,1)}, u32[]{:S(2)}, u32[]{:S(2)}) collective-permute-start(bf16[1024,256]{1,0:T(8,128)(2,1)} %get-tuple-element.41), channel_id=1, source_target_pairs={{1,2},{2,1},{5,6},{6,5},{9,10},{10,9},{13,14},{14,13},{17,18},{18,... | collective-permute-start | bytes 1572872 | tf_op jit(solution)/shard_map/ppermute | solution.py:85
  41.7 9.5 %copy-start.11 = (bf16[256,256]{1,0:T(8,128)(2,1)S(1)}, bf16[256,256]{1,0:T(8,128)(2,1)}, u32[]{:S(2)}) copy-start(bf16[256,256]{1,0:T(8,128)(2,1)} %copy-done.10) | copy-start | bytes 393220
  43.3 8.8 %copy-start.6 = (bf16[1024,256]{1,0:T(8,128)(2,1)S(1)}, bf16[1024,256]{1,0:T(8,128)(2,1)}, u32[]{:S(2)}) copy-start(bf16[1024,256]{1,0:T(8,128)(2,1)} %copy-done.5) | copy-start | bytes 1572868
  43.3 18.1 %collective-permute-start.8 = (bf16[1024,256]{1,0:T(8,128)(2,1)S(1)}, bf16[1024,256]{1,0:T(8,128)(2,1)S(1)}, u32[]{:S(2)}, u32[]{:S(2)}) collective-permute-start(bf16[1024,256]{1,0:T(8,128)(2,1)S(1)} %select_select_fusion.3), channel_id=1, source_target_pairs={{0,1},{1,0},{2,3},{3,2},{4,5},{5,4},{6,7},{7,6},{8,9},{9,8},{10,11... | collective-permute-start | bytes 1572872 | tf_op jit(solution)/shard_map/ppermute | solution.py:18
  51.3 10.1 %copy-start.4 = (bf16[1024,256]{1,0:T(8,128)(2,1)S(1)}, bf16[1024,256]{1,0:T(8,128)(2,1)}, u32[]{:S(2)}) copy-start(bf16[1024,256]{1,0:T(8,128)(2,1)} %copy-done.3) | copy-start | bytes 1572868
  51.3 17.6 %collective-permute-start.9 = (bf16[1024,256]{1,0:T(8,128)(2,1)S(1)}, bf16[1024,256]{1,0:T(8,128)(2,1)S(1)}, u32[]{:S(2)}, u32[]{:S(2)}) collective-permute-start(bf16[1024,256]{1,0:T(8,128)(2,1)S(1)} %get-tuple-element.61), channel_id=1, source_target_pairs={{1,2},{2,1},{5,6},{6,5},{9,10},{10,9},{13,14},{14,13},{17,18},{18,... | collective-permute-start | bytes 1572872 | tf_op jit(solution)/shard_map/ppermute | solution.py:98
  53.7 16.7 %collective-permute-start.7 = (bf16[1024,256]{1,0:T(8,128)(2,1)S(1)}, bf16[1024,256]{1,0:T(8,128)(2,1)S(1)}, u32[]{:S(2)}, u32[]{:S(2)}) collective-permute-start(bf16[1024,256]{1,0:T(8,128)(2,1)S(1)} %get-tuple-element.44), channel_id=1, source_target_pairs={{1,2},{2,1},{5,6},{6,5},{9,10},{10,9},{13,14},{14,13},{17,18},{18,... | collective-permute-start | bytes 1572872 | tf_op jit(solution)/shard_map/ppermute | solution.py:115
  63.7 26.7 %copy-start.7 = (bf16[256,1024]{1,0:T(8,128)(2,1)}, bf16[256,1024]{1,0:T(8,128)(2,1)S(1)}, u32[]{:S(2)}) copy-start(bf16[256,1024]{1,0:T(8,128)(2,1)S(1)} %convolution_convert_fusion.2) | copy-start | bytes 1572868
  63.7 17.6 %collective-permute-start.10 = (bf16[256,1024]{1,0:T(8,128)(2,1)S(1)}, bf16[256,1024]{1,0:T(8,128)(2,1)S(1)}, u32[]{:S(2)}, u32[]{:S(2)}) collective-permute-start(bf16[256,1024]{1,0:T(8,128)(2,1)S(1)} %convolution_convert_fusion.2), channel_id=1, source_target_pairs={{0,1},{1,0},{2,3},{3,2},{4,5},{5,4},{6,7},{7,6},{8,9},{9,8},{10,11... | collective-permute-start | bytes 1572872 | tf_op jit(solution)/shard_map/ppermute | solution.py:18
  69.1 21.2 %collective-permute-start.11 = (bf16[1024,256]{1,0:T(8,128)(2,1)S(1)}, bf16[1024,256]{1,0:T(8,128)(2,1)S(1)}, u32[]{:S(2)}, u32[]{:S(2)}) collective-permute-start(bf16[1024,256]{1,0:T(8,128)(2,1)S(1)} %broadcast_select_fusion.8), channel_id=1, source_target_pairs={{1,0},{2,3},{5,4},{6,7},{9,8},{10,11},{13,12},{14,15},{17,16},{18,... | collective-permute-start | bytes 1572872 | tf_op jit(solution)/shard_map/ppermute | solution.py:119
  81.3 9.0 %copy-start.8 = (bf16[256,1024]{1,0:T(8,128)(2,1)}, bf16[256,1024]{1,0:T(8,128)(2,1)S(1)}, u32[]{:S(2)}) copy-start(bf16[256,1024]{1,0:T(8,128)(2,1)S(1)} %collective-permute-done.10) | copy-start | bytes 1572868
  82.7 23.5 %collective-permute-start.12 = (bf16[256,1024]{1,0:T(8,128)(2,1)}, bf16[256,1024]{1,0:T(8,128)(2,1)}, u32[]{:S(2)}, u32[]{:S(2)}) collective-permute-start(bf16[256,1024]{1,0:T(8,128)(2,1)} %fusion.2), channel_id=1, source_target_pairs={{0,2},{1,3},{2,0},{3,1},{4,6},{5,7},{6,4},{7,5},{8,10},{9,11},{10,... | collective-permute-start | bytes 1572872 | tf_op jit(solution)/shard_map/ppermute | solution.py:18
  92.6 16.6 %all-to-all-start.1 = ((bf16[8,48,1024]{2,1,0:T(8,128)(2,1)}), bf16[8,48,1024]{2,1,0:T(8,128)(2,1)S(1)}, u32[]{:S(2)}, u32[]{:S(2)}) async-start(bf16[8,48,1024]{2,1,0:T(8,128)(2,1)} %bitcast.61), calls=%async_computation.1 | async-start | bytes 1572864 | tf_op jit(solution)/shard_map/all_to_all | solution.py:260
  (9 other events, 25.6 us)
